TPU v7x, 256 devices: a whole 4x4x8 slice. The times are simulated.
256 devices in a mesh: space: 8 (over z_hi, y), dp: 32 (over x, z_lo, core).
Axes of the slice: x: 4, y: 4, z: 8 (z_hi: 2, z_lo: 4; z = z_hi * 4 + z_lo), core: 2. Of those that a mesh axis runs over, the one named last changes fastest.
Arguments:
- features: bfloat16 [32, 48, 64, 8, 128], P('dp', None, 'space'), may hold values from -21 to 21
- upstream: bfloat16 [32, 48, 64, 8, 128], P('dp', None, 'space'), may hold values from -21 to 21
- weight_one: bfloat16 [48, 48, 3, 3, 3], replicated, may hold values from -0.15625 to 0.15625
- weight_two: bfloat16 [48, 48, 3, 3, 3], replicated, may hold values from -0.15625 to 0.15625
- norm_gain: float32 [48], replicated, may hold values from 0.25 to 1.75
- norm_bias: float32 [48], replicated, may hold values from -3 to 3
Outputs:
- grad_input: bfloat16 [32, 48, 64, 8, 128], P('dp', None, 'space')
- grad_one: float32 [48, 48, 3, 3, 3], replicated
- grad_two: float32 [48, 48, 3, 3, 3], replicated
- grad_gain: float32 [48], replicated
- grad_bias: float32 [48], replicated
All inputs are finite; a program needn't handle non-finite values.
Results may differ from a plain program's by a relative error of at most 0.0029.
Values may be sent and summed in bfloat16 or wider, within the bound.
A program may use at most 128 MiB of HBM per device.

v0:
```python
import jax
import jax.numpy as jnp
from jax import lax
from jax.sharding import PartitionSpec as P

epsilon = 1e-05


def padded_2(cells, sides, width):
    for axis, dim in sides:
        count = lax.axis_size(axis)
        ends = count - 1
        head = lax.slice_in_dim(cells, 0, width, axis=dim)
        tail = lax.slice_in_dim(cells, cells.shape[dim] - width, cells.shape[dim], axis=dim)
        cells = jnp.concatenate(
            [
                lax.ppermute(tail, axis, [(i, (i + 1) % count) for i in range(ends)]),
                cells,
                lax.ppermute(head, axis, [((i + 1) % count, i) for i in range(ends)]),
            ],
            axis=dim,
        )
    return cells


def slab_faces(field):
    return padded_2(field, (("space", 2),), 1)


def conv_slab(padded, kernel):
    return lax.conv_general_dilated(
        padded,
        kernel,
        (1, 1, 1),
        ((0, 0), (1, 1), (1, 1)),
        dimension_numbers=("NCDHW", "OIDHW", "NCDHW"),
        preferred_element_type=jnp.float32,
    )


def flipped(kernel):
    return jnp.transpose(kernel, (1, 0, 2, 3, 4))[:, :, ::-1, ::-1, ::-1]


def kernel_grad(padded, target):
    return lax.conv_general_dilated(
        padded,
        target,
        (1, 1, 1),
        ((0, 0), (1, 1), (1, 1)),
        dimension_numbers=("CNDHW", "IODHW", "CNDHW"),
        preferred_element_type=jnp.float32,
    )


def local(features, upstream, weight_one, weight_two, norm_gain, norm_bias):
    axes_cells = (2, 3, 4)
    cells_all = float(
        features.shape[2] * features.shape[3] * features.shape[4] * lax.axis_size("space")
    )
    padded_x = slab_faces(features)
    pre_act = conv_slab(padded_x, weight_one)
    sums_pre, squares_pre = lax.psum(
        (
            jnp.sum(pre_act, axis=axes_cells, keepdims=True),
            jnp.sum(pre_act * pre_act, axis=axes_cells, keepdims=True),
        ),
        "space",
    )
    mean_pre = sums_pre / cells_all
    inv_std = lax.rsqrt(squares_pre / cells_all - mean_pre * mean_pre + epsilon)
    normal_hat = (pre_act - mean_pre) * inv_std
    gain_b = norm_gain.reshape(1, -1, 1, 1, 1)
    normed = normal_hat * gain_b + norm_bias.reshape(1, -1, 1, 1, 1)
    sigmoid_val = jax.nn.sigmoid(normed)
    hidden = (normed * sigmoid_val).astype(jnp.bfloat16)
    padded_h = slab_faces(hidden)
    padded_g = slab_faces(upstream)
    local_two = kernel_grad(padded_h, upstream)
    grad_hidden = conv_slab(padded_g, flipped(weight_two))
    grad_norm = grad_hidden * sigmoid_val * (1.0 + normed * (1.0 - sigmoid_val))
    local_bias = jnp.sum(grad_norm, axis=(0, 2, 3, 4))
    local_gain = jnp.sum(grad_norm * normal_hat, axis=(0, 2, 3, 4))
    slope_sum, slope_dot = lax.psum(
        (
            jnp.sum(grad_norm, axis=axes_cells, keepdims=True),
            jnp.sum(grad_norm * normal_hat, axis=axes_cells, keepdims=True),
        ),
        "space",
    )
    grad_pre = (
        gain_b
        * inv_std
        * (grad_norm - slope_sum / cells_all - normal_hat * (slope_dot / cells_all))
    ).astype(jnp.bfloat16)
    padded_grad = slab_faces(grad_pre)
    local_one = kernel_grad(padded_x, grad_pre)
    back = conv_slab(padded_grad, flipped(weight_one))
    grad_input = (upstream.astype(jnp.float32) + back).astype(jnp.bfloat16)
    grad_one, grad_two, grad_gain, grad_bias = lax.psum(
        (local_one, local_two, local_gain, local_bias), ("space", "dp")
    )
    return (grad_input, grad_one, grad_two, grad_gain, grad_bias)


def solution(mesh):
    in_specs = (
        P("dp", None, "space", None, None),
        P("dp", None, "space", None, None),
        P(),
        P(),
        P(),
        P(),
    )
    out_specs = (P("dp", None, "space", None, None), P(), P(), P(), P())
    return jax.shard_map(local, mesh=mesh, in_specs=in_specs, out_specs=out_specs, check_vma=False)
```

profile of v0, /device:TPU:1, one launch (start us, length us, event | category | flops | bytes accessed | tf_op | source)
XLA Modules:
  0.0 684.3 jit_solution(1534281291638809892)
XLA Ops:
  8.3 4.2 collective-permute-start
  15.4 4.6 collective-permute-start.2
  21.3 7.4 %copy.112 = bf16[1,48,8,8,128]{1,0,4,3,2:T(2,128)(2,1)} copy(bf16[1,48,8,8,128]{4,3,2,1,0:T(8,128)(2,1)} %param.7) | data formatting | bytes 1572864 | tf_op args[1]
  28.7 2.5 copy.85
  31.3 3.5 copy.86
  34.8 3.6 fusion.70
  38.4 3.1 fusion.68
  44.4 2.0 pad_maximum_fusion.3
  46.5 4.9 copy.89
  51.3 2.3 pad.2
  56.6 12.1 %select_reduce_fusion.3 = (f32[48]{0:T(128)S(1)}, f32[48]{0:T(128)S(1)}, f32[8,8,8,17,48]{4,2,3,1,0:T(8,128)}) fusion(pred[8,17]{0,1:T(8,128)(4,1)S(1)} %copy-done.14, bf16[48,48,3,3,3]{1,0,4,3,2:T(8,128)(2,1)S(1)} %copy-done, bf16[48,10,8,1,7,2]{0,4,5,2,1,3:T(8,128)(2,1)S(1)} %copy-done.13, bf16[48,10,8,1,8,17]{0,4,5,2,1,3:T(8,128)(2,1)S(1)} %copy-done.11), kind=kOutput, calls=%fused_computation.25 | convolution fusion | flops 998682496 | bytes 2948104 | tf_op jit(solution)/shard_map/conv_general_dilated | solution.py:31
  68.7 30.8 %all-reduce.3 = (f32[1,48,1,1,1]{1,4,3,2,0:T(1,128)S(1)}, f32[1,48,1,1,1]{1,4,3,2,0:T(1,128)S(1)}) all-reduce(f32[1,48,1,1,1]{1,4,3,2,0:T(1,128)S(1)} %bitcast.113, f32[1,48,1,1,1]{1,4,3,2,0:T(1,128)S(1)} %bitcast.112), channel_id=1, replica_groups=mesh['space'=8,'dp'=32] {'space'}, use_global_device_ids=true, to_apply=%region_1.0 | all-reduce | flops 96 | bytes 768 | tf_op jit(solution)/shard_map/psum | solution.py:63
  99.5 16.4 %select_reduce_fusion = (f32[48]{0:T(128)S(1)}, f32[48]{0:T(128)S(1)}, f32[8,8,8,17,48]{4,2,3,1,0:T(8,128)}) fusion(pred[8,17]{0,1:T(8,128)(4,1)S(1)} %copy-done.14, f32[48]{0:T(128)S(1)} %bitcast.108, f32[48]{0:T(128)S(1)} %get-tuple-element.55, f32[8,8,8,17,48]{4,2,3,1,0:T(8,128)} %get-tuple-element.56, f32[48]{0:T(128)S(1)} %copy-done.16, ...), kind=kOutput, calls=%fused_computation.17 | convolution fusion | flops 1004113792 | bytes 4620040 | tf_op jit(solution)/shard_map/conv_general_dilated | solution.py:31
  115.9 25.0 %all-reduce.2 = (f32[1,48,1,1,1]{1,4,3,2,0:T(1,128)S(1)}, f32[1,48,1,1,1]{1,4,3,2,0:T(1,128)S(1)}) all-reduce(f32[1,48,1,1,1]{1,4,3,2,0:T(1,128)S(1)} %bitcast.111, f32[1,48,1,1,1]{1,4,3,2,0:T(1,128)S(1)} %bitcast.110), channel_id=1, replica_groups=mesh['space'=8,'dp'=32] {'space'}, use_global_device_ids=true, to_apply=%region_5.0 | all-reduce | flops 96 | bytes 768 | tf_op jit(solution)/shard_map/psum | solution.py:84
  140.9 4.9 multiply_convert_fusion.1
  147.5 2.2 collective-permute-start.6
  152.3 2.3 copy.117
  154.6 2.3 copy.118
  156.9 1.9 copy.104
  159.0 4.0 collective-permute-start.4
  165.9 17.9 %fusion.49 = f32[48,48,3,3,3]{0,1,4,3,2:T(8,128)} fusion(bf16[8,8,8,17,48]{4,2,3,1,0:T(8,128)(2,1)S(1)} %get-tuple-element.40, pred[8,17]{0,1:T(8,128)(4,1)S(1)} %copy-done.14, bf16[48,10,8,8,17,1]{0,3,5,4,2,1:T(8,128)(2,1)S(1)} %get-tuple-element.60, bf16[48,10,8,8,17,1]{0,3,5,4,2,1:T(8,128)(2,1)} %copy.104, ...), kind=kOutput, calls=%fused_computation.61 | convolution fusion | flops 1002491904 | bytes 4217992 | tf_op jit(solution)/shard_map/conv_general_dilated | solution.py:46
  184.3 6.4 copy.126
  190.7 101.2 %all-reduce = (f32[48]{0:T(128)}, f32[48]{0:T(128)}) all-reduce(f32[48]{0:T(128)S(1)} %get-tuple-element.25, f32[48]{0:T(128)S(1)} %get-tuple-element.26), channel_id=1, replica_groups=mesh['space'=8,'dp'=32] {'space','dp'}, use_global_device_ids=true, to_apply=%region_10.0 | all-reduce | flops 96 | bytes 768 | tf_op jit(solution)/shard_map/psum | solution.py:100
  293.7 10.5 %broadcast_select_fusion = f32[8,8,8,17,48]{4,2,3,1,0:T(8,128)S(1)} fusion(pred[8,17]{0,1:T(8,128)(4,1)S(1)} %copy-done.14, bf16[48,48,3,3,3]{1,0,4,3,2:T(8,128)(2,1)S(1)} %copy-done, bf16[48,10,8,1,7,2]{0,4,5,2,1,3:T(8,128)(2,1)S(1)} %slice.57, bf16[48,10,8,1,8,17]{0,4,5,2,1,3:T(8,128)(2,1)S(1)} %copy.98), kind=kOutput, calls=%fused_computation.55 | convolution fusion | flops 996593664 | bytes 2947720 | tf_op jit(solution)/shard_map/conv_general_dilated | solution.py:31
  304.2 3.1 copy.99
  307.4 1.8 copy-done.8
  309.3 110.6 %fusion.11 = f32[48,48,3,3,3]{0,1,4,3,2:T(8,128)} fusion(bf16[1,48,8,8,128]{1,0,4,3,2:T(2,128)(2,1)S(1)} %copy-done.7, bf16[1,48,1,8,128]{1,0,4,3,2:T(2,128)(2,1)} %collective-permute-done.7, bf16[1,48,8,8,128]{1,0,4,3,2:T(2,128)(2,1)S(1)} %bitcast.102, bf16[1,48,1,8,128]{1,0,4,3,2:T(2,128)(2,1)} %collective-permute-done.6), kind=kOutput, calls=%fused_computation.15 | convolution fusion | flops 932364288 | bytes 2018304 | tf_op jit(solution)/shard_map/conv_general_dilated | solution.py:46
  419.9 4.1 fusion.13
  424.0 3.8 copy.113
  427.8 245.1 %all-reduce.6.cloned.1.call-done = (f32[48,48,3,3,3]{0,1,4,3,2:T(8,128)}, f32[48,48,3,3,3]{0,1,4,3,2:T(8,128)}) async-done(((f32[48,48,3,3,3]{0,1,4,3,2:T(8,128)}, f32[48,48,3,3,3]{0,1,4,3,2:T(8,128)}), (f32[48,48,3,3,3]{0,1,4,3,2:T(8,128)}, f32[48,48,3,3,3]{0,1,4,3,2:T(8,128)})) %all-reduce.6.cloned.1.call-update) | async-done | bytes 497680 | tf_op jit(solution)/shard_map/psum | solution.py:100
  672.9 2.2 copy.114
  675.1 2.2 copy.115
  (80 shorter events, 20.8 us)
Async XLA Ops:
  7.2 47.9 %copy-start = (bf16[48,48,3,3,3]{1,0,4,3,2:T(8,128)(2,1)S(1)}, bf16[48,48,3,3,3]{1,0,4,3,2:T(8,128)(2,1)}, u32[]{:S(2)}) copy-start(bf16[48,48,3,3,3]{1,0,4,3,2:T(8,128)(2,1)} %param.8) | copy-start | bytes 373252
  7.2 21.5 %copy-start.5 = (bf16[1,48,8,8,128]{4,3,2,1,0:T(8,128)(2,1)S(1)}, bf16[1,48,8,8,128]{4,3,2,1,0:T(8,128)(2,1)}, u32[]{:S(2)}) copy-start(bf16[1,48,8,8,128]{4,3,2,1,0:T(8,128)(2,1)} %param.7) | copy-start | bytes 2359300
  7.2 665.7 %all-reduce.6.cloned.1.call-start = ((), (), s32[]{:S(2)}) async-start(), calls=%async_computation | async-start | bytes 2654208 | tf_op jit(solution)/shard_map/psum | solution.py:100
  8.3 22.9 %copy-start.12 = (bf16[1,48,8,8,128]{4,3,2,1,0:T(8,128)(2,1)S(1)}, bf16[1,48,8,8,128]{4,3,2,1,0:T(8,128)(2,1)}, u32[]{:S(2)}) copy-start(bf16[1,48,8,8,128]{4,3,2,1,0:T(8,128)(2,1)} %param.6) | copy-start | bytes 2359300
  8.3 22.9 %collective-permute-start = (bf16[1,48,1,8,128]{4,3,2,1,0:T(8,128)(2,1)S(1)}, bf16[1,48,1,8,128]{4,3,2,1,0:T(8,128)(2,1)S(1)}, u32[]{:S(2)}, u32[]{:S(2)}) collective-permute-start(bf16[1,48,1,8,128]{4,3,2,1,0:T(8,128)(2,1)S(1)} %get-tuple-element.51), channel_id=1, source_target_pairs={{0,32},{32,64},{64,96},{96,128},{128,160},{160,192},{192,224},{1,3... | collective-permute-start | bytes 294920 | tf_op jit(solution)/shard_map/ppermute | solution.py:17
  12.5 18.7 %collective-permute-start.1 = (bf16[1,48,1,8,128]{4,3,2,1,0:T(8,128)(2,1)S(1)}, bf16[1,48,1,8,128]{4,3,2,1,0:T(8,128)(2,1)S(1)}, u32[]{:S(2)}, u32[]{:S(2)}) collective-permute-start(bf16[1,48,1,8,128]{4,3,2,1,0:T(8,128)(2,1)S(1)} %get-tuple-element.52), channel_id=1, source_target_pairs={{32,0},{64,32},{96,64},{128,96},{160,128},{192,160},{224,192},{33,... | collective-permute-start | bytes 294920 | tf_op jit(solution)/shard_map/ppermute | solution.py:19
  15.4 29.1 %collective-permute-start.2 = (bf16[1,48,1,8,128]{4,3,2,1,0:T(8,128)(2,1)}, bf16[1,48,1,8,128]{4,3,2,1,0:T(8,128)(2,1)}, u32[]{:S(2)}, u32[]{:S(2)}) collective-permute-start(bf16[1,48,1,8,128]{4,3,2,1,0:T(8,128)(2,1)} %get-tuple-element.53), channel_id=1, source_target_pairs={{0,32},{32,64},{64,96},{96,128},{128,160},{160,192},{192,224},{1,3... | collective-permute-start | bytes 294920 | tf_op jit(solution)/shard_map/ppermute | solution.py:17
  20.0 24.4 %collective-permute-start.3 = (bf16[1,48,1,8,128]{4,3,2,1,0:T(8,128)(2,1)S(1)}, bf16[1,48,1,8,128]{4,3,2,1,0:T(8,128)(2,1)}, u32[]{:S(2)}, u32[]{:S(2)}) collective-permute-start(bf16[1,48,1,8,128]{4,3,2,1,0:T(8,128)(2,1)S(1)} %get-tuple-element.54), channel_id=1, source_target_pairs={{32,0},{64,32},{96,64},{128,96},{160,128},{192,160},{224,192},{33,... | collective-permute-start | bytes 294920 | tf_op jit(solution)/shard_map/ppermute | solution.py:19
  41.5 2.9 copy-start.6
  42.1 1.6 copy-start.10
  53.7 2.6 copy-start.11
  53.7 2.8 copy-start.13
  53.7 2.8 copy-start.14
  54.2 14.5 %copy-start.9 = (bf16[48,10,8,1,8,17]{0,4,5,2,1,3:T(8,128)(2,1)}, bf16[48,10,8,1,8,17]{0,4,5,2,1,3:T(8,128)(2,1)S(1)}, u32[]{:S(2)}) copy-start(bf16[48,10,8,1,8,17]{0,4,5,2,1,3:T(8,128)(2,1)S(1)} %copy.91) | copy-start | bytes 3133444
  56.5 43.0 %copy-start.15 = (f32[48]{0:T(128)S(1)}, f32[48]{0:T(128)}, u32[]{:S(2)}) copy-start(f32[48]{0:T(128)} %param.10) | copy-start | bytes 580
  56.5 43.0 %copy-start.16 = (f32[48]{0:T(128)S(1)}, f32[48]{0:T(128)}, u32[]{:S(2)}) copy-start(f32[48]{0:T(128)} %param.11) | copy-start | bytes 580
  145.8 6.5 copy-start.3
  146.2 8.3 %copy-start.2 = (bf16[48,10,8,1,8,16]{0,2,5,4,1,3:T(8,128)(2,1)S(1)}, bf16[48,10,8,1,8,16]{0,2,5,4,1,3:T(8,128)(2,1)}, u32[]{:S(2)}) copy-start(bf16[48,10,8,1,8,16]{0,2,5,4,1,3:T(8,128)(2,1)} %get-tuple-element.42) | copy-start | bytes 2949124
  147.5 159.8 %collective-permute-start.6 = (bf16[1,48,1,8,128]{1,0,4,3,2:T(2,128)(2,1)}, bf16[1,48,1,8,128]{1,0,4,3,2:T(2,128)(2,1)}, u32[]{:S(2)}, u32[]{:S(2)}) collective-permute-start(bf16[1,48,1,8,128]{1,0,4,3,2:T(2,128)(2,1)} %bitcast.90), channel_id=1, source_target_pairs={{0,32},{32,64},{64,96},{96,128},{128,160},{160,192},{192,224},{1,3... | collective-permute-start | bytes 294920 | tf_op jit(solution)/shard_map/ppermute | solution.py:17
  151.0 156.3 %collective-permute-start.7 = (bf16[1,48,1,8,128]{1,0,4,3,2:T(2,128)(2,1)}, bf16[1,48,1,8,128]{1,0,4,3,2:T(2,128)(2,1)}, u32[]{:S(2)}, u32[]{:S(2)}) collective-permute-start(bf16[1,48,1,8,128]{1,0,4,3,2:T(2,128)(2,1)} %bitcast.89), channel_id=1, source_target_pairs={{32,0},{64,32},{96,64},{128,96},{160,128},{192,160},{224,192},{33,... | collective-permute-start | bytes 294920 | tf_op jit(solution)/shard_map/ppermute | solution.py:19
  159.0 132.9 %collective-permute-start.4 = (bf16[1,48,1,8,128]{1,3,4,0,2:T(8,128)(2,1)S(1)}, bf16[1,48,1,8,128]{1,3,4,0,2:T(8,128)(2,1)S(1)}, u32[]{:S(2)}, u32[]{:S(2)}) collective-permute-start(bf16[1,48,1,8,128]{1,3,4,0,2:T(8,128)(2,1)S(1)} %slice_bitcast_fusion.3), channel_id=1, source_target_pairs={{0,32},{32,64},{64,96},{96,128},{128,160},{160,192},{192,224},{1,3... | collective-permute-start | bytes 294920 | tf_op jit(solution)/shard_map/ppermute | solution.py:17
  163.0 128.9 %collective-permute-start.5 = (bf16[1,48,1,8,128]{1,3,4,2,0:T(8,128)(2,1)S(1)}, bf16[1,48,1,8,128]{1,3,4,2,0:T(8,128)(2,1)S(1)}, u32[]{:S(2)}, u32[]{:S(2)}) collective-permute-start(bf16[1,48,1,8,128]{1,3,4,2,0:T(8,128)(2,1)S(1)} %slice_bitcast_fusion.2), channel_id=1, source_target_pairs={{32,0},{64,32},{96,64},{128,96},{160,128},{192,160},{224,192},{33,... | collective-permute-start | bytes 294920 | tf_op jit(solution)/shard_map/ppermute | solution.py:19
  304.2 3.3 copy-start.7
  304.2 5.1 copy-start.8
  309.2 110.6 %copy-start.4 = (bf16[1,48,8,8,128]{1,3,4,2,0:T(8,128)(2,1)S(1)}, bf16[1,48,8,8,128]{1,3,4,2,0:T(8,128)(2,1)}, u32[]{:S(2)}) copy-start(bf16[1,48,8,8,128]{1,3,4,2,0:T(8,128)(2,1)} %copy.85) | copy-start | bytes 2359300
  419.9 257.4 %copy-start.1 = (bf16[48,48,3,3,3]{1,0,4,3,2:T(8,128)(2,1)S(1)}, bf16[48,48,3,3,3]{1,0,4,3,2:T(8,128)(2,1)}, u32[]{:S(2)}) copy-start(bf16[48,48,3,3,3]{1,0,4,3,2:T(8,128)(2,1)} %param.8) | copy-start | bytes 373252
Sparse Core Ops, SparseCore 0:
  420.0 252.9 all-reduce.5
where the time goes:
time: 690 us; the launch traced here: 684 us
  waiting for transfers between devices  245 us (36%)
  matrix products  167 us (24%)
  blocking collectives  157 us (23%)
  local copies, waits for them, and re-layouts  66.6 us (10%)
  starting transfers between devices  20.2 us (3%)
  between operations  14.7 us (2%)
  other arithmetic  13.3 us (2%)
    psum x1, waiting for transfers between devices, local(): lax.psum((local_one, local_two, local_gain, local_bias), ('space', 'dp'))  245 us
    conv_general_dilated x2, matrix products, kernel_grad(): lax.conv_general_dilated(padded, target, (1, 1, 1), ((0, 0), (1, 1), (1,...  128 us
    psum x1, blocking collectives, local(): lax.psum((local_one, local_two, local_gain, local_bias), ('space', 'dp'))  101 us
    conv_general_dilated x3, matrix products, conv_slab(): lax.conv_general_dilated(padded, kernel, (1, 1, 1), ((0, 0), (1, 1), (1,...  39 us
    unnamed x46, local copies, waits for them, and re-layouts  36.6 us
    psum x1, blocking collectives, local(): lax.psum((jnp.sum(pre_act, axis=axes_cells, keepdims=True), jnp.sum(pre_a...  30.8 us
    psum x1, blocking collectives, local(): lax.psum((jnp.sum(grad_norm, axis=axes_cells, keepdims=True), jnp.sum(gra...  25 us
    concatenate x8, local copies, waits for them, and re-layouts, padded_2(): jnp.concatenate([lax.ppermute(tail, axis, [(i, (i + 1) % count) for i in...  20 us
  transfers between devices with their start and end apart: 9, of which 1 were waited for; matrix products, arithmetic and copies ran while one was open for 12% of the time, Pallas kernels for 0%

commit v1 on v0

--- a/solution.py
+++ b/solution.py
@@ -98,7 +98,7 @@
     back = conv_slab(padded_grad, flipped(weight_one))
     grad_input = (upstream.astype(jnp.float32) + back).astype(jnp.bfloat16)
     grad_one, grad_two, grad_gain, grad_bias = lax.psum(
-        (local_one, local_two, local_gain, local_bias), ("space", "dp")
+        lax.psum((local_one, local_two, local_gain, local_bias), "dp"), "space"
     )
     return (grad_input, grad_one, grad_two, grad_gain, grad_bias)
 

time: 690 us -> 766 us (1.11)
  waiting for transfers between devices: 245 us -> 386 us
  matrix products: 167 us -> 130 us
  blocking collectives: 157 us -> 129 us
    psum x1 -> x2, waiting for transfers between devices: 245 us -> 386 us  [the longest x1 285 us: local(): lax.psum((local_one, local_two, local_gain, local_bias), 'dp')]
    conv_general_dilated x2, matrix products: 128 us -> 91.3 us  [kernel_grad(): lax.conv_general_dilated(padded, target, (1, 1, 1), ((0, 0), (1, 1), (1,...]
    psum x1, blocking collectives: 101 us -> 72.3 us  [local(): lax.psum((local_one, local_two, local_gain, local_bias), 'dp')]
    unnamed x46 -> x48, local copies, waits for them, and re-layouts: 36.6 us -> 34.2 us
  transfers between devices with their start and end apart: 9 -> 10, of which waited for: 1 -> 2; matrix products, arithmetic and copies ran while one was open for 12% -> 20% of each run, Pallas kernels for 0% -> 0%
where the time goes in v1:
time: 766 us; the launch traced here: 756 us
  waiting for transfers between devices  386 us (50%)
  matrix products  130 us (17%)
  blocking collectives  129 us (17%)
  local copies, waits for them, and re-layouts  65 us (8%)
  starting transfers between devices  21 us (3%)
  between operations  14.9 us (2%)
  other arithmetic  10.6 us (1%)
    psum x1, waiting for transfers between devices, local(): lax.psum((local_one, local_two, local_gain, local_bias), 'dp')  285 us
    psum x1, waiting for transfers between devices, local(): lax.psum(lax.psum((local_one, local_two, local_gain, local_bias), 'dp'),...  101 us
    conv_general_dilated x2, matrix products, kernel_grad(): lax.conv_general_dilated(padded, target, (1, 1, 1), ((0, 0), (1, 1), (1,...  91.3 us
    psum x1, blocking collectives, local(): lax.psum((local_one, local_two, local_gain, local_bias), 'dp')  72.3 us
    conv_general_dilated x3, matrix products, conv_slab(): lax.conv_general_dilated(padded, kernel, (1, 1, 1), ((0, 0), (1, 1), (1,...  38.6 us
    unnamed x48, local copies, waits for them, and re-layouts  34.2 us
    psum x1, blocking collectives, local(): lax.psum((jnp.sum(pre_act, axis=axes_cells, keepdims=True), jnp.sum(pre_a...  30.6 us
    psum x1, blocking collectives, local(): lax.psum((jnp.sum(grad_norm, axis=axes_cells, keepdims=True), jnp.sum(gra...  25.8 us
  transfers between devices with their start and end apart: 10, of which 2 were waited for; matrix products, arithmetic and copies ran while one was open for 20% of the time, Pallas kernels for 0%

profile of v1, /device:TPU:1, one launch (start us, length us, event | category | flops | bytes accessed | tf_op | source)
XLA Modules:
  0.0 756.5 jit_solution(9780317928570091704)
XLA Ops:
  8.3 4.2 collective-permute-start
  15.4 4.6 collective-permute-start.2
  21.3 7.4 copy.112
  28.7 2.5 copy.85
  31.4 3.5 copy.86
  34.8 3.6 fusion.70
  38.4 3.2 fusion.68
  44.5 2.0 pad_maximum_fusion.3
  46.5 5.1 copy.89
  51.6 2.3 pad.2
  56.8 12.2 %select_reduce_fusion.3 = (f32[48]{0:T(128)S(1)}, f32[48]{0:T(128)S(1)}, f32[8,8,8,17,48]{4,2,3,1,0:T(8,128)}) fusion(pred[8,17]{0,1:T(8,128)(4,1)S(1)} %copy-done.14, bf16[48,48,3,3,3]{1,0,4,3,2:T(8,128)(2,1)S(1)} %copy-done, bf16[48,10,8,1,7,2]{0,4,5,2,1,3:T(8,128)(2,1)S(1)} %copy-done.13, bf16[48,10,8,1,8,17]{0,4,5,2,1,3:T(8,128)(2,1)S(1)} %copy-done.10), kind=kOutput, calls=%fused_computation.25 | convolution fusion | flops 998682496 | bytes 2948104 | tf_op jit(solution)/shard_map/conv_general_dilated | solution.py:31
  69.0 30.6 %all-reduce.3 = (f32[1,48,1,1,1]{1,4,3,2,0:T(1,128)S(1)}, f32[1,48,1,1,1]{1,4,3,2,0:T(1,128)S(1)}) all-reduce(f32[1,48,1,1,1]{1,4,3,2,0:T(1,128)S(1)} %bitcast.112, f32[1,48,1,1,1]{1,4,3,2,0:T(1,128)S(1)} %bitcast.111), channel_id=1, replica_groups=mesh['space'=8,'dp'=32] {'space'}, use_global_device_ids=true, to_apply=%region_1.0 | all-reduce | flops 96 | bytes 768 | tf_op jit(solution)/shard_map/psum | solution.py:63
  99.6 16.4 %select_reduce_fusion = (f32[48]{0:T(128)S(1)}, f32[48]{0:T(128)S(1)}, f32[8,8,8,17,48]{4,2,3,1,0:T(8,128)}) fusion(pred[8,17]{0,1:T(8,128)(4,1)S(1)} %copy-done.14, f32[48]{0:T(128)S(1)} %bitcast.107, f32[48]{0:T(128)S(1)} %get-tuple-element.59, f32[8,8,8,17,48]{4,2,3,1,0:T(8,128)} %get-tuple-element.60, f32[48]{0:T(128)S(1)} %copy-done.17, ...), kind=kOutput, calls=%fused_computation.17 | convolution fusion | flops 1004113792 | bytes 4620040 | tf_op jit(solution)/shard_map/conv_general_dilated | solution.py:31
  116.0 72.3 %all-reduce = (f32[48]{0:T(128)S(1)}, f32[48]{0:T(128)S(1)}) all-reduce(f32[48]{0:T(128)S(1)} %get-tuple-element.25, f32[48]{0:T(128)S(1)} %get-tuple-element.26), channel_id=1, replica_groups=mesh['space'=8,'dp'=32] {'dp'}, use_global_device_ids=true, to_apply=%region_12.0 | all-reduce | flops 96 | bytes 768 | tf_op jit(solution)/shard_map/psum | solution.py:101
  188.2 25.8 %all-reduce.2 = (f32[1,48,1,1,1]{1,4,3,2,0:T(1,128)S(1)}, f32[1,48,1,1,1]{1,4,3,2,0:T(1,128)S(1)}, f32[48]{0:T(128)}, f32[48]{0:T(128)}) all-reduce(f32[1,48,1,1,1]{1,4,3,2,0:T(1,128)S(1)} %bitcast.110, f32[1,48,1,1,1]{1,4,3,2,0:T(1,128)S(1)} %bitcast.109, f32[48]{0:T(128)S(1)} %get-tuple-element.29, ...), channel_id=1, replica_groups=mesh['space'=8,'dp'=32] {'space'}, use_global_device_ids=true, to_apply=%region_5.0 | all-reduce | flops 192 | bytes 1536 | tf_op jit(solution)/shard_map/psum | solution.py:84
  214.0 4.9 multiply_convert_fusion.1
  218.9 1.7 copy.93
  222.0 2.1 collective-permute-start.6
  226.6 2.3 copy.117
  228.9 2.3 copy.118
  231.3 1.9 copy.104
  234.0 4.7 collective-permute-start.4
  242.6 16.3 %fusion.49 = f32[48,48,3,3,3]{0,1,4,3,2:T(8,128)} fusion(bf16[8,8,8,17,48]{4,2,3,1,0:T(8,128)(2,1)S(1)} %get-tuple-element.44, pred[8,17]{0,1:T(8,128)(4,1)S(1)} %copy-done.14, bf16[48,10,8,8,17,1]{0,3,5,4,2,1:T(8,128)(2,1)S(1)} %get-tuple-element.64, bf16[48,10,8,8,17,1]{0,3,5,4,2,1:T(8,128)(2,1)S(1)} %copy-done.11, ...), kind=kOutput, calls=%fused_computation.61 | convolution fusion | flops 1002491904 | bytes 4217992 | tf_op jit(solution)/shard_map/conv_general_dilated | solution.py:46
  259.3 6.3 copy.126
  265.7 75.0 %fusion.11 = f32[48,48,3,3,3]{0,1,4,3,2:T(8,128)} fusion(bf16[1,48,8,8,128]{1,0,4,3,2:T(2,128)(2,1)S(1)} %copy-done.7, bf16[1,48,1,8,128]{1,0,4,3,2:T(2,128)(2,1)} %collective-permute-done.7, bf16[1,48,8,8,128]{1,0,4,3,2:T(2,128)(2,1)} %bitcast.102, bf16[1,48,1,8,128]{1,0,4,3,2:T(2,128)(2,1)} %collective-permute-done.6), kind=kOutput, calls=%fused_computation.15 | convolution fusion | flops 932364288 | bytes 2018304 | tf_op jit(solution)/shard_map/conv_general_dilated | solution.py:46
  340.9 1.6 maximum_bitcast_fusion
  343.7 285.0 %all-reduce.8.cloned.1.call-done = (f32[48,48,3,3,3]{0,1,4,3,2:T(8,128)}, f32[48,48,3,3,3]{0,1,4,3,2:T(8,128)}) async-done(((f32[48,48,3,3,3]{0,1,4,3,2:T(8,128)}, f32[48,48,3,3,3]{0,1,4,3,2:T(8,128)}), (f32[48,48,3,3,3]{0,1,4,3,2:T(8,128)}, f32[48,48,3,3,3]{0,1,4,3,2:T(8,128)})) %all-reduce.8.cloned.1.call-update) | async-done | bytes 497680 | tf_op jit(solution)/shard_map/psum | solution.py:101
  628.7 10.1 %broadcast_select_fusion = f32[8,8,8,17,48]{4,2,3,1,0:T(8,128)S(1)} fusion(pred[8,17]{0,1:T(8,128)(4,1)S(1)} %copy-done.15, bf16[48,48,3,3,3]{1,0,4,3,2:T(8,128)(2,1)S(1)} %copy-done, bf16[48,10,8,1,7,2]{0,4,5,2,1,3:T(8,128)(2,1)S(1)} %slice.57, bf16[48,10,8,1,8,17]{0,4,5,2,1,3:T(8,128)(2,1)S(1)} %copy.98), kind=kOutput, calls=%fused_computation.55 | convolution fusion | flops 996593664 | bytes 2947720 | tf_op jit(solution)/shard_map/conv_general_dilated | solution.py:31
  640.9 2.7 copy.113
  643.5 101.4 %all-reduce.10.cloned.1.call-done = (f32[48,48,3,3,3]{0,1,4,3,2:T(8,128)}, f32[48,48,3,3,3]{0,1,4,3,2:T(8,128)}) async-done(((f32[48,48,3,3,3]{0,1,4,3,2:T(8,128)}, f32[48,48,3,3,3]{0,1,4,3,2:T(8,128)}), (f32[48,48,3,3,3]{0,1,4,3,2:T(8,128)}, f32[48,48,3,3,3]{0,1,4,3,2:T(8,128)})) %all-reduce.10.cloned.1.call-update) | async-done | bytes 497680 | tf_op jit(solution)/shard_map/psum | solution.py:100
  744.9 2.2 copy.114
  747.1 2.2 copy.115
  (85 shorter events, 23.4 us)
Async XLA Ops:
  7.2 48.2 %copy-start = (bf16[48,48,3,3,3]{1,0,4,3,2:T(8,128)(2,1)S(1)}, bf16[48,48,3,3,3]{1,0,4,3,2:T(8,128)(2,1)}, u32[]{:S(2)}) copy-start(bf16[48,48,3,3,3]{1,0,4,3,2:T(8,128)(2,1)} %param.8) | copy-start | bytes 373252
  7.2 21.5 %copy-start.5 = (bf16[1,48,8,8,128]{4,3,2,1,0:T(8,128)(2,1)S(1)}, bf16[1,48,8,8,128]{4,3,2,1,0:T(8,128)(2,1)}, u32[]{:S(2)}) copy-start(bf16[1,48,8,8,128]{4,3,2,1,0:T(8,128)(2,1)} %param.7) | copy-start | bytes 2359300
  7.2 621.5 %all-reduce.8.cloned.1.call-start = ((), (), s32[]{:S(2)}) async-start(), calls=%async_computation | async-start | bytes 2654208 | tf_op jit(solution)/shard_map/psum | solution.py:101
  8.3 22.9 %copy-start.12 = (bf16[1,48,8,8,128]{4,3,2,1,0:T(8,128)(2,1)S(1)}, bf16[1,48,8,8,128]{4,3,2,1,0:T(8,128)(2,1)}, u32[]{:S(2)}) copy-start(bf16[1,48,8,8,128]{4,3,2,1,0:T(8,128)(2,1)} %param.6) | copy-start | bytes 2359300
  8.3 22.9 %collective-permute-start = (bf16[1,48,1,8,128]{4,3,2,1,0:T(8,128)(2,1)S(1)}, bf16[1,48,1,8,128]{4,3,2,1,0:T(8,128)(2,1)S(1)}, u32[]{:S(2)}, u32[]{:S(2)}) collective-permute-start(bf16[1,48,1,8,128]{4,3,2,1,0:T(8,128)(2,1)S(1)} %get-tuple-element.55), channel_id=1, source_target_pairs={{0,32},{32,64},{64,96},{96,128},{128,160},{160,192},{192,224},{1,3... | collective-permute-start | bytes 294920 | tf_op jit(solution)/shard_map/ppermute | solution.py:17
  12.5 18.8 %collective-permute-start.1 = (bf16[1,48,1,8,128]{4,3,2,1,0:T(8,128)(2,1)S(1)}, bf16[1,48,1,8,128]{4,3,2,1,0:T(8,128)(2,1)S(1)}, u32[]{:S(2)}, u32[]{:S(2)}) collective-permute-start(bf16[1,48,1,8,128]{4,3,2,1,0:T(8,128)(2,1)S(1)} %get-tuple-element.56), channel_id=1, source_target_pairs={{32,0},{64,32},{96,64},{128,96},{160,128},{192,160},{224,192},{33,... | collective-permute-start | bytes 294920 | tf_op jit(solution)/shard_map/ppermute | solution.py:19
  15.4 29.1 %collective-permute-start.2 = (bf16[1,48,1,8,128]{4,3,2,1,0:T(8,128)(2,1)}, bf16[1,48,1,8,128]{4,3,2,1,0:T(8,128)(2,1)}, u32[]{:S(2)}, u32[]{:S(2)}) collective-permute-start(bf16[1,48,1,8,128]{4,3,2,1,0:T(8,128)(2,1)} %get-tuple-element.57), channel_id=1, source_target_pairs={{0,32},{32,64},{64,96},{96,128},{128,160},{160,192},{192,224},{1,3... | collective-permute-start | bytes 294920 | tf_op jit(solution)/shard_map/ppermute | solution.py:17
  20.0 24.5 %collective-permute-start.3 = (bf16[1,48,1,8,128]{4,3,2,1,0:T(8,128)(2,1)S(1)}, bf16[1,48,1,8,128]{4,3,2,1,0:T(8,128)(2,1)}, u32[]{:S(2)}, u32[]{:S(2)}) collective-permute-start(bf16[1,48,1,8,128]{4,3,2,1,0:T(8,128)(2,1)S(1)} %get-tuple-element.58), channel_id=1, source_target_pairs={{32,0},{64,32},{96,64},{128,96},{160,128},{192,160},{224,192},{33,... | collective-permute-start | bytes 294920 | tf_op jit(solution)/shard_map/ppermute | solution.py:19
  41.6 2.9 copy-start.6
  42.1 1.5 copy-start.9
  54.0 2.6 copy-start.10
  54.0 2.8 copy-start.13
  54.0 2.8 copy-start.14
  54.5 14.5 %copy-start.8 = (bf16[48,10,8,1,8,17]{0,4,5,2,1,3:T(8,128)(2,1)}, bf16[48,10,8,1,8,17]{0,4,5,2,1,3:T(8,128)(2,1)S(1)}, u32[]{:S(2)}) copy-start(bf16[48,10,8,1,8,17]{0,4,5,2,1,3:T(8,128)(2,1)S(1)} %copy.91) | copy-start | bytes 3133444
  56.8 42.7 %copy-start.16 = (f32[48]{0:T(128)S(1)}, f32[48]{0:T(128)}, u32[]{:S(2)}) copy-start(f32[48]{0:T(128)} %param.10) | copy-start | bytes 580
  56.8 42.8 %copy-start.17 = (f32[48]{0:T(128)S(1)}, f32[48]{0:T(128)}, u32[]{:S(2)}) copy-start(f32[48]{0:T(128)} %param.11) | copy-start | bytes 580
  218.9 7.7 %copy-start.2 = (bf16[48,10,8,1,8,16]{0,2,5,4,1,3:T(8,128)(2,1)S(1)}, bf16[48,10,8,1,8,16]{0,2,5,4,1,3:T(8,128)(2,1)}, u32[]{:S(2)}) copy-start(bf16[48,10,8,1,8,16]{0,2,5,4,1,3:T(8,128)(2,1)} %get-tuple-element.45) | copy-start | bytes 2949124
  220.8 8.2 %copy-start.1 = (bf16[48,10,8,1,8,16]{0,2,5,4,1,3:T(8,128)(2,1)S(1)}, bf16[48,10,8,1,8,16]{0,2,5,4,1,3:T(8,128)(2,1)}, u32[]{:S(2)}) copy-start(bf16[48,10,8,1,8,16]{0,2,5,4,1,3:T(8,128)(2,1)} %get-tuple-element.46) | copy-start | bytes 2949124
  222.0 43.6 %collective-permute-start.6 = (bf16[1,48,1,8,128]{1,0,4,3,2:T(2,128)(2,1)}, bf16[1,48,1,8,128]{1,0,4,3,2:T(2,128)(2,1)}, u32[]{:S(2)}, u32[]{:S(2)}) collective-permute-start(bf16[1,48,1,8,128]{1,0,4,3,2:T(2,128)(2,1)} %bitcast.90), channel_id=1, source_target_pairs={{0,32},{32,64},{64,96},{96,128},{128,160},{160,192},{192,224},{1,3... | collective-permute-start | bytes 294920 | tf_op jit(solution)/shard_map/ppermute | solution.py:17
  225.3 40.3 %collective-permute-start.7 = (bf16[1,48,1,8,128]{1,0,4,3,2:T(2,128)(2,1)}, bf16[1,48,1,8,128]{1,0,4,3,2:T(2,128)(2,1)}, u32[]{:S(2)}, u32[]{:S(2)}) collective-permute-start(bf16[1,48,1,8,128]{1,0,4,3,2:T(2,128)(2,1)} %bitcast.89), channel_id=1, source_target_pairs={{32,0},{64,32},{96,64},{128,96},{160,128},{192,160},{224,192},{33,... | collective-permute-start | bytes 294920 | tf_op jit(solution)/shard_map/ppermute | solution.py:19
  234.0 106.9 %collective-permute-start.4 = (bf16[1,48,1,8,128]{1,3,4,0,2:T(8,128)(2,1)}, bf16[1,48,1,8,128]{1,3,4,0,2:T(8,128)(2,1)}, u32[]{:S(2)}, u32[]{:S(2)}) collective-permute-start(bf16[1,48,1,8,128]{1,3,4,0,2:T(8,128)(2,1)} %slice_bitcast_fusion.3), channel_id=1, source_target_pairs={{0,32},{32,64},{64,96},{96,128},{128,160},{160,192},{192,224},{1,3... | collective-permute-start | bytes 294920 | tf_op jit(solution)/shard_map/ppermute | solution.py:17
  239.5 3.1 copy-start.11
  239.5 101.5 %collective-permute-start.5 = (bf16[1,48,1,8,128]{1,3,4,2,0:T(8,128)(2,1)}, bf16[1,48,1,8,128]{1,3,4,2,0:T(8,128)(2,1)}, u32[]{:S(2)}, u32[]{:S(2)}) collective-permute-start(bf16[1,48,1,8,128]{1,3,4,2,0:T(8,128)(2,1)} %slice_bitcast_fusion.2), channel_id=1, source_target_pairs={{32,0},{64,32},{96,64},{128,96},{160,128},{192,160},{224,192},{33,... | collective-permute-start | bytes 294920 | tf_op jit(solution)/shard_map/ppermute | solution.py:19
  259.3 6.3 copy-start.7
  265.6 75.1 %copy-start.3 = (bf16[8,8,8,17,48]{4,1,3,2,0:T(8,128)(2,1)S(1)}, bf16[8,8,8,17,48]{4,1,3,2,0:T(8,128)(2,1)}, u32[]{:S(2)}) copy-start(bf16[8,8,8,17,48]{4,1,3,2,0:T(8,128)(2,1)} %copy.93) | copy-start | bytes 2506756
  340.7 404.2 %all-reduce.10.cloned.1.call-start = ((), (), s32[]{:S(2)}) async-start(), calls=%async_computation.1 | async-start | bytes 2654208 | tf_op jit(solution)/shard_map/psum | solution.py:100
  343.1 285.6 %copy-start.15 = (pred[8,17]{0,1:T(8,128)(4,1)S(1)}, pred[8,17]{0,1:T(8,128)(4,1)}, u32[]{:S(2)}) copy-start(pred[8,17]{0,1:T(8,128)(4,1)} %constant.35) | copy-start | bytes 412
  638.8 1.6 copy-start.4
Sparse Core Ops, SparseCore 0:
  340.8 287.8 all-reduce.7
  631.7 113.2 all-reduce.9
